TPU v7x, 512 devices: a whole 4x8x8 slice. The times are simulated.
512 devices in a mesh: leaf: 32 (over y, x), row: 8 (over z), col: 2 (over core).
Axes of the slice: x: 4, y: 8, z: 8, core: 2. Of those that a mesh axis runs over, the one named last changes fastest.
Arguments:
- leaf_update: float32 [32, 512, 512], P('leaf', 'row', 'col'), as said below
- leaf_rhs: float32 [32, 512, 256], P('leaf', 'row', 'col'), may hold values from -6 to 6
- child_rows: int32 [31, 2, 512], replicated, may hold values from 0 to 1023, as said below
- separator_coef: float32 [31, 512], replicated, may hold values from 0.5 to 4
Outputs:
- final_update: float32 [512, 512], P('row', 'col')
- final_rhs: float32 [512, 256], P('row', 'col')
- separator_solutions: float32 [32, 512, 256], P('leaf', 'row', 'col')
Inputs may be any that keep to these rules, and one draw needn't show every extreme that they name: Each child_rows[f, c] lists 512 distinct rows of the front. Each leaf_update[i] is symmetric positive definite.
All inputs are finite; a program needn't handle non-finite values.
Results may differ from a plain program's by a relative error of at most 0.00017.
Values sent between devices are 32-bit elements; how exact they have to be, the bound alone decides.
A program may use at most 128 MiB of HBM per device.

v0:
```python
import jax
import jax.numpy as jnp
from jax import lax
from jax.sharding import PartitionSpec as P


def from_partner(block, axis, apart):
    count = lax.axis_size(axis)
    route = []
    for low in range(count):
        high = low | 1 << apart
        if high != low and high < count:
            route += [(low, high), (high, low)]
    return lax.ppermute(block, axis, route)


def stencil_block(sep_coefs):
    positions = jnp.arange(sep_coefs.shape[0], dtype=jnp.int32)
    distance = positions[:, None] - positions[None, :]
    return jnp.where(
        distance == 0, sep_coefs[:, None] + 2.0, jnp.where(jnp.abs(distance) == 1, -1.0, 0.0)
    )


def matmul_high(left, right):
    return jnp.dot(left, right, precision=lax.Precision.HIGHEST)


def factor_inverse(matrix):
    order = matrix.shape[0]
    if order <= 32:
        lower_factor = jnp.linalg.cholesky(matrix)
        identity = jnp.eye(order, dtype=matrix.dtype)
        return jax.scipy.linalg.solve_triangular(lower_factor, identity, lower=True)
    half = order // 2
    inv_top = factor_inverse(matrix[:half, :half])
    lower_left = matmul_high(matrix[half:, :half], inv_top.T)
    schur_part = matrix[half:, half:] - matmul_high(lower_left, lower_left.T)
    inv_bottom = factor_inverse(schur_part)
    inv_left = -matmul_high(inv_bottom, matmul_high(lower_left, inv_top))
    upper_rows = jnp.concatenate([inv_top, jnp.zeros((half, order - half), matrix.dtype)], axis=1)
    lower_rows = jnp.concatenate([inv_left, inv_bottom], axis=1)
    return jnp.concatenate([upper_rows, lower_rows], axis=0)


def inverse_map(mapping, front_size):
    sources = jnp.arange(mapping.shape[0], dtype=jnp.int32)
    return jnp.full((front_size,), -1, jnp.int32).at[mapping].set(sources)


def spread_rows(full_rows, inverse, parent_rows):
    source = inverse[parent_rows]
    present = source >= 0
    picked = jnp.take(full_rows, jnp.maximum(source, 0), axis=0)
    return jnp.where(present[:, None], picked, 0.0)


def spread_block(full_matrix, inverse, parent_rows, parent_cols):
    src_rows = inverse[parent_rows]
    src_cols = inverse[parent_cols]
    picked = jnp.take(
        jnp.take(full_matrix, jnp.maximum(src_rows, 0), axis=0), jnp.maximum(src_cols, 0), axis=1
    )
    present = (src_rows >= 0)[:, None] & (src_cols >= 0)[None, :]
    return jnp.where(present, picked, 0.0)


def per_device(leaf_update, leaf_rhs, child_rows, separator_coef):
    update_blk = leaf_update[0]
    rhs_blk = leaf_rhs[0]
    leaf_count = lax.axis_size("leaf")
    row_count = lax.axis_size("row")
    col_count = lax.axis_size("col")
    levels = leaf_count.bit_length() - 1
    leaf_index = lax.axis_index("leaf")
    row_index = lax.axis_index("row")
    col_index = lax.axis_index("col")
    row_block, col_block = update_blk.shape
    rhs_cols = rhs_blk.shape[1]
    update_size = row_block * row_count
    sep_size = separator_coef.shape[1]
    front_size = sep_size + update_size
    sep_rows = jnp.arange(sep_size, dtype=jnp.int32)
    own_rows = sep_size + row_index * row_block + jnp.arange(row_block, dtype=jnp.int32)
    own_cols = sep_size + col_index * col_block + jnp.arange(col_block, dtype=jnp.int32)
    sep_share = sep_size // row_count
    kept_rows = jnp.zeros((sep_share, rhs_cols), jnp.float32)
    offset = 0
    for level_no in range(1, levels + 1):
        bit_no = level_no - 1
        other_upd, other_rhs = from_partner((update_blk, rhs_blk), "leaf", bit_no)
        blocks = lax.all_gather(
            jnp.stack([update_blk, other_upd])[:, None], ("row", "col"), axis=1, tiled=True
        )
        whole_rhs = lax.all_gather(jnp.stack([rhs_blk, other_rhs]), "row", axis=1, tiled=True)
        whole_upd = (
            blocks.reshape(2, row_count, col_count, row_block, col_block)
            .transpose(0, 1, 3, 2, 4)
            .reshape(2, update_size, update_size)
        )
        own_upd, partner_upd = (whole_upd[0], whole_upd[1])
        own_rhs, partner_rhs = (whole_rhs[0], whole_rhs[1])
        out_rows, out_cols = (own_rows, own_cols)
        upper_half = leaf_index >> bit_no & 1 == 1
        first_upd = jnp.where(upper_half, partner_upd, own_upd)
        second_upd = jnp.where(upper_half, own_upd, partner_upd)
        first_rhs = jnp.where(upper_half, partner_rhs, own_rhs)
        second_rhs = jnp.where(upper_half, own_rhs, partner_rhs)
        front_id = offset + (leaf_index >> level_no)
        mapping = lax.dynamic_index_in_dim(child_rows, front_id, 0, keepdims=False)
        sep_coefs = lax.dynamic_index_in_dim(separator_coef, front_id, 0, keepdims=False)
        inv_first = inverse_map(mapping[0], front_size)
        inv_second = inverse_map(mapping[1], front_size)

        def assemble(parent_rows, parent_cols):
            return spread_block(first_upd, inv_first, parent_rows, parent_cols) + spread_block(
                second_upd, inv_second, parent_rows, parent_cols
            )

        diag_block = stencil_block(sep_coefs) + assemble(sep_rows, sep_rows)
        factor_inv = factor_inverse(diag_block)
        panel_rows = matmul_high(factor_inv, assemble(out_rows, sep_rows).T)
        panel_cols = matmul_high(factor_inv, assemble(out_cols, sep_rows).T)
        update_blk = assemble(out_rows, out_cols) - matmul_high(panel_rows.T, panel_cols)
        rhs_sep = spread_rows(first_rhs, inv_first, sep_rows) + spread_rows(
            second_rhs, inv_second, sep_rows
        )
        rhs_own = spread_rows(first_rhs, inv_first, out_rows) + spread_rows(
            second_rhs, inv_second, out_rows
        )
        solved = matmul_high(factor_inv, rhs_sep)
        rhs_blk = rhs_own - matmul_high(panel_rows.T, solved)
        store_here = leaf_index & (1 << level_no) - 1 == 1 << bit_no
        if level_no == levels:
            store_here = store_here | (leaf_index & (1 << bit_no) - 1 == 0)
        kept_rows = jnp.where(
            store_here,
            lax.dynamic_slice_in_dim(solved, row_index * sep_share, sep_share, 0),
            kept_rows,
        )
        offset += leaf_count >> level_no
    return (update_blk, rhs_blk, kept_rows[None])


def solution(mesh):
    in_specs = (P("leaf", "row", "col"), P("leaf", "row", "col"), P(), P())
    out_specs = (P("row", "col"), P("row", "col"), P("leaf", "row", "col"))
    return jax.shard_map(
        per_device, mesh=mesh, in_specs=in_specs, out_specs=out_specs, check_vma=False
    )
```

profile of v0, /device:TPU:56, one launch (start us, length us, event | category | flops | bytes accessed | tf_op | source)
XLA Modules:
  0.0 1204.7 jit_solution(3808599444853935362)
XLA Ops:
  7.2 3.4 collective-permute-start
  10.6 3.0 collective-permute-done
  21.3 3.0 scatter_custom_fusion.5
  35.0 27.5 %all-gather.11.cloned.1.call-done = f32[2,1024,256]{2,1,0:T(8,128)} async-done(((f32[2,64,256]{2,1,0:T(8,128)}), f32[2,1024,256]{2,1,0:T(8,128)}) %all-gather.11.cloned.1.call-update) | async-done | bytes 2097168 | tf_op jit(solution)/shard_map/all_gather | solution.py:92
  62.5 3.2 copy.566
  98.4 2.9 cholesky.1225
  129.8 2.9 cholesky.1269
  145.3 2.9 cholesky.1291
  177.8 3.1 cholesky.1335
  193.8 2.9 cholesky.1357
  224.9 4.9 collective-permute-start.1
  259.6 15.1 %all-gather.13.cloned.1.call-done = f32[2,1024,256]{2,1,0:T(8,128)} async-done(((f32[2,64,256]{2,1,0:T(8,128)}), f32[2,1024,256]{2,1,0:T(8,128)}) %all-gather.13.cloned.1.call-update) | async-done | bytes 2097168 | tf_op jit(solution)/shard_map/all_gather | solution.py:92
  310.6 2.9 cholesky.1401
  342.1 2.9 cholesky.1445
  357.7 2.9 cholesky.1467
  375.4 2.9 cholesky.1489
  391.0 3.1 cholesky.1511
  407.1 2.9 cholesky.1533
  438.1 3.4 collective-permute-start.2
  445.0 3.4 collective-permute-start.5
  482.3 4.1 all-gather.15.cloned.1.call-done
  522.7 2.9 cholesky.1577
  554.7 2.9 cholesky.1621
  604.1 3.1 cholesky.1687
  620.4 2.9 cholesky.1709
  651.4 4.2 collective-permute-start.3
  656.2 3.6 collective-permute-done.3
  674.3 26.1 %all_gather.35 = f32[2,512,128]{2,1,0:T(8,128)S(1)} all-gather(f32[2,64,128]{2,1,0:T(8,128)S(1)} %pad_maximum_fusion.5), channel_id=1, replica_groups=mesh['leaf'=32,'row'=8,'col'=2] {'row'}, dimensions={1}, use_global_device_ids=true | all-gather | bytes 589824 | tf_op jit(solution)/shard_map/all_gather | solution.py:95
  706.8 5.2 collective-permute-start.6
  747.3 2.9 cholesky.1753
  811.8 2.9 cholesky.1841
  827.4 3.3 cholesky.1863
  843.6 2.9 cholesky.1885
  874.3 5.0 collective-permute-start.4
  880.2 4.4 collective-permute-done.4
  885.2 26.0 %all_gather.36 = f32[2,512,128]{2,1,0:T(8,128)S(1)} all-gather(f32[2,64,128]{2,1,0:T(8,128)S(1)} %pad_maximum_fusion.6), channel_id=1, replica_groups=mesh['leaf'=32,'row'=8,'col'=2] {'row'}, dimensions={1}, use_global_device_ids=true | all-gather | bytes 589824 | tf_op jit(solution)/shard_map/all_gather | solution.py:95
  918.6 3.9 collective-permute-done.7
  922.4 25.7 %all_gather.37 = f32[2,512,128]{2,1,0:T(8,128)S(1)} all-gather(f32[2,64,128]{2,1,0:T(8,128)S(1)} %pad_maximum_fusion.7), channel_id=1, replica_groups=mesh['leaf'=32,'row'=8,'col'=2] {'row'}, dimensions={1}, use_global_device_ids=true | all-gather | bytes 589824 | tf_op jit(solution)/shard_map/all_gather | solution.py:95
  953.6 3.2 collective-permute-start.8
  956.8 3.5 collective-permute-done.8
  960.3 25.3 %all_gather.38 = f32[2,512,128]{2,1,0:T(8,128)S(1)} all-gather(f32[2,64,128]{2,1,0:T(8,128)S(1)} %pad_maximum_fusion.8), channel_id=1, replica_groups=mesh['leaf'=32,'row'=8,'col'=2] {'row'}, dimensions={1}, use_global_device_ids=true | all-gather | bytes 589824 | tf_op jit(solution)/shard_map/all_gather | solution.py:95
  991.2 5.0 collective-permute-start.9
  996.3 5.0 collective-permute-done.9
  1001.3 25.2 %all_gather.39 = f32[2,512,128]{2,1,0:T(8,128)S(1)} all-gather(f32[2,64,128]{2,1,0:T(8,128)S(1)} %pad_maximum_fusion.9), channel_id=1, replica_groups=mesh['leaf'=32,'row'=8,'col'=2] {'row'}, dimensions={1}, use_global_device_ids=true | all-gather | bytes 589824 | tf_op jit(solution)/shard_map/all_gather | solution.py:95
  1099.1 2.9 cholesky.1973
  1114.6 2.9 cholesky.1995
  1147.1 3.1 cholesky.2039
  1163.1 2.9 cholesky.2061
  (1930 shorter events, 870.5 us)
Async XLA Ops:
  7.2 55.3 %all-gather.11.cloned.1.call-start = ((), (), s32[]{:S(2)}) async-start(), calls=%async_computation | async-start | bytes 2228224 | tf_op jit(solution)/shard_map/all_gather | solution.py:92
  7.2 6.4 collective-permute-start
  15.1 259.6 %all-gather.13.cloned.1.call-start = ((), (), s32[]{:S(2)}) async-start(), calls=%async_computation.1 | async-start | bytes 2228224 | tf_op jit(solution)/shard_map/all_gather | solution.py:92
  31.0 180.8 %copy-start.89 = (s32[1024]{0:T(1024)}, s32[1024]{0:T(1024)S(1)}, u32[]{:S(2)}) copy-start(s32[1024]{0:T(1024)S(1)} %pad_clamp_fusion.24) | copy-start | bytes 12292
  31.7 178.2 %copy-start.91 = (s32[1024]{0:T(1024)}, s32[1024]{0:T(1024)S(1)}, u32[]{:S(2)}) copy-start(s32[1024]{0:T(1024)S(1)} %pad_clamp_fusion.25) | copy-start | bytes 12292
  31.7 35.0 %copy-start.144 = (s32[1024]{0:T(1024)}, s32[1024]{0:T(1024)S(1)}, u32[]{:S(2)}) copy-start(s32[1024]{0:T(1024)S(1)} %pad_clamp_fusion.30) | copy-start | bytes 12292
  33.8 33.6 %copy-start.198 = (pred[64]{0:T(512)(128)(4,1)}, pred[64]{0:T(512)(128)(4,1)S(1)}, u32[]{:S(2)}) copy-start(pred[64]{0:T(512)(128)(4,1)S(1)} %get-tuple-element.167) | copy-start | bytes 196
  153.0 69.9 %copy-start.25 = (f32[256,256]{1,0:T(8,128)}, f32[256,256]{1,0:T(8,128)S(1)}, u32[]{:S(2)}) copy-start(f32[256,256]{1,0:T(8,128)S(1)} %select_maximum_fusion.9) | copy-start | bytes 786436
  154.5 54.8 %copy-start.24 = (f32[256,64]{1,0:T(8,128)S(1)}, f32[256,64]{1,0:T(8,128)}, u32[]{:S(2)}) copy-start(f32[256,64]{1,0:T(8,128)} %gather_fusion.33) | copy-start | bytes 196612
  162.2 47.3 %copy-start = (f32[256,512]{1,0:T(8,128)S(1)}, f32[256,512]{1,0:T(8,128)}, u32[]{:S(2)}) copy-start(f32[256,512]{1,0:T(8,128)} %gather_fusion.40) | copy-start | bytes 1572868
  162.2 47.3 %copy-start.226 = (pred[256]{0:T(512)(128)(4,1)S(1)}, pred[256]{0:T(512)(128)(4,1)}, u32[]{:S(2)}) copy-start(pred[256]{0:T(512)(128)(4,1)} %get-tuple-element.143) | copy-start | bytes 772
  224.9 7.7 collective-permute-start.1
  233.2 253.1 %all-gather.15.cloned.1.call-start = ((), (), s32[]{:S(2)}) async-start(), calls=%async_computation.2 | async-start | bytes 2228224 | tf_op jit(solution)/shard_map/all_gather | solution.py:92
  251.9 24.5 %copy-start.132 = (s32[256]{0:T(256)}, s32[256]{0:T(256)S(1)}, u32[]{:S(2)}) copy-start(s32[256]{0:T(256)S(1)} %gather_fusion.5) | copy-start | bytes 3076
  255.9 169.2 %copy-start.93 = (s32[1024]{0:T(1024)}, s32[1024]{0:T(1024)S(1)}, u32[]{:S(2)}) copy-start(s32[1024]{0:T(1024)S(1)} %pad_clamp_fusion.18) | copy-start | bytes 12292
  257.2 24.2 %copy-start.95 = (s32[1024]{0:T(1024)}, s32[1024]{0:T(1024)S(1)}, u32[]{:S(2)}) copy-start(s32[1024]{0:T(1024)S(1)} %pad_clamp_fusion.19) | copy-start | bytes 12292
  365.4 70.8 %copy-start.27 = (f32[256,256]{1,0:T(8,128)}, f32[256,256]{1,0:T(8,128)S(1)}, u32[]{:S(2)}) copy-start(f32[256,256]{1,0:T(8,128)S(1)} %select_maximum_fusion.8) | copy-start | bytes 786436
  367.6 55.0 %copy-start.18 = (f32[256,64]{1,0:T(8,128)S(1)}, f32[256,64]{1,0:T(8,128)}, u32[]{:S(2)}) copy-start(f32[256,64]{1,0:T(8,128)} %gather_fusion.45) | copy-start | bytes 196612
  375.0 47.8 %copy-start.1 = (f32[256,512]{1,0:T(8,128)S(1)}, f32[256,512]{1,0:T(8,128)}, u32[]{:S(2)}) copy-start(f32[256,512]{1,0:T(8,128)} %gather_fusion.54) | copy-start | bytes 1572868
  375.0 47.8 %copy-start.223 = (pred[256]{0:T(512)(128)(4,1)S(1)}, pred[256]{0:T(512)(128)(4,1)}, u32[]{:S(2)}) copy-start(pred[256]{0:T(512)(128)(4,1)} %get-tuple-element.82) | copy-start | bytes 772
  438.1 6.2 collective-permute-start.2
  444.9 267.1 %all-gather.17.cloned.1.call-start = ((), (), s32[]{:S(2)}) async-start(), calls=%async_computation.3 | async-start | bytes 2228224 | tf_op jit(solution)/shard_map/all_gather | solution.py:92
  445.0 228.6 %collective-permute-start.5 = (f32[64,128]{1,0:T(8,128)}, f32[64,128]{1,0:T(8,128)}, u32[]{:S(2)}, u32[]{:S(2)}) collective-permute-start(f32[64,128]{1,0:T(8,128)} %bitcast.331), channel_id=1, source_target_pairs={{0,16},{16,0},{32,48},{48,32},{64,80},{80,64},{96,112},{112,96},{1... | collective-permute-start | bytes 98312 | tf_op jit(solution)/shard_map/ppermute | solution.py:14
  452.7 27.1 %copy-start.128 = (s32[256]{0:T(256)}, s32[256]{0:T(256)S(1)}, u32[]{:S(2)}) copy-start(s32[256]{0:T(256)S(1)} %gather_fusion.1) | copy-start | bytes 3076
  455.0 26.0 %copy-start.116 = (s32[512]{0:T(512)}, s32[512]{0:T(512)S(1)}, u32[]{:S(2)}) copy-start(s32[512]{0:T(512)S(1)} %gather_fusion.28) | copy-start | bytes 6148
  578.3 71.3 %copy-start.29 = (f32[256,256]{1,0:T(8,128)}, f32[256,256]{1,0:T(8,128)S(1)}, u32[]{:S(2)}) copy-start(f32[256,256]{1,0:T(8,128)S(1)} %select_maximum_fusion.7) | copy-start | bytes 786436
  580.5 55.6 %copy-start.19 = (f32[256,64]{1,0:T(8,128)S(1)}, f32[256,64]{1,0:T(8,128)}, u32[]{:S(2)}) copy-start(f32[256,64]{1,0:T(8,128)} %gather_fusion.59) | copy-start | bytes 196612
  587.9 48.3 %copy-start.2 = (f32[256,512]{1,0:T(8,128)S(1)}, f32[256,512]{1,0:T(8,128)}, u32[]{:S(2)}) copy-start(f32[256,512]{1,0:T(8,128)} %gather_fusion.68) | copy-start | bytes 1572868
  587.9 48.3 %copy-start.219 = (pred[256]{0:T(512)(128)(4,1)S(1)}, pred[256]{0:T(512)(128)(4,1)}, u32[]{:S(2)}) copy-start(pred[256]{0:T(512)(128)(4,1)} %get-tuple-element.145) | copy-start | bytes 772
  651.4 8.5 collective-permute-start.3
  660.5 371.8 %all-gather.19.cloned.1.call-start = ((), (), s32[]{:S(2)}) async-start(), calls=%async_computation.4 | async-start | bytes 2228224 | tf_op jit(solution)/shard_map/all_gather | solution.py:92
  664.1 37.0 %copy-start.92 = (s32[1024]{0:T(1024)S(1)}, s32[1024]{0:T(1024)}, u32[]{:S(2)}) copy-start(s32[1024]{0:T(1024)} %copy-done.91) | copy-start | bytes 12292
  670.0 48.1 %copy-start.108 = (s32[1024]{0:T(1024)}, s32[1024]{0:T(1024)S(1)}, u32[]{:S(2)}) copy-start(s32[1024]{0:T(1024)S(1)} %pad_clamp_fusion.7) | copy-start | bytes 12292
  670.6 44.7 %copy-start.214 = (pred[64]{0:T(512)(128)(4,1)}, pred[64]{0:T(512)(128)(4,1)S(1)}, u32[]{:S(2)}) copy-start(pred[64]{0:T(512)(128)(4,1)S(1)} %get-tuple-element.155) | copy-start | bytes 196
  673.5 41.1 %copy-start.147 = (s32[1024]{0:T(1024)}, s32[1024]{0:T(1024)S(1)}, u32[]{:S(2)}) copy-start(s32[1024]{0:T(1024)S(1)} %pad_clamp_fusion.11) | copy-start | bytes 12292
  706.8 172.6 %collective-permute-start.6 = (f32[64,128]{1,0:T(8,128)}, f32[64,128]{1,0:T(8,128)}, u32[]{:S(2)}, u32[]{:S(2)}) collective-permute-start(f32[64,128]{1,0:T(8,128)} %convolution_subtract_fusion.44), channel_id=1, source_target_pairs={{0,32},{32,0},{16,48},{48,16},{64,96},{96,64},{80,112},{112,80},{1... | collective-permute-start | bytes 98312 | tf_op jit(solution)/shard_map/ppermute | solution.py:14
  811.4 47.8 %copy-start.3 = (f32[256,512]{1,0:T(8,128)S(1)}, f32[256,512]{1,0:T(8,128)}, u32[]{:S(2)}) copy-start(f32[256,512]{1,0:T(8,128)} %gather_fusion.82) | copy-start | bytes 1572868
  811.4 47.8 %copy-start.221 = (pred[256]{0:T(512)(128)(4,1)S(1)}, pred[256]{0:T(512)(128)(4,1)}, u32[]{:S(2)}) copy-start(pred[256]{0:T(512)(128)(4,1)} %get-tuple-element.74) | copy-start | bytes 772
  873.9 38.0 %copy-start.98 = (s32[1024]{0:T(1024)S(1)}, s32[1024]{0:T(1024)}, u32[]{:S(2)}) copy-start(s32[1024]{0:T(1024)} %copy-done.95) | copy-start | bytes 12292
  874.3 10.2 collective-permute-start.4
  916.3 31.9 %copy-start.15 = (f32[512,128]{1,0:T(8,128)}, f32[512,128]{1,0:T(8,128)S(1)}, u32[]{:S(2)}) copy-start(f32[512,128]{1,0:T(8,128)S(1)} %fusion.306) | copy-start | bytes 786436
  916.3 32.6 %copy-start.106 = (s32[1024]{0:T(1024)S(1)}, s32[1024]{0:T(1024)}, u32[]{:S(2)}) copy-start(s32[1024]{0:T(1024)} %copy-done.103) | copy-start | bytes 12292
  916.6 5.8 collective-permute-start.7
  953.3 32.4 %copy-start.16 = (f32[512,128]{1,0:T(8,128)}, f32[512,128]{1,0:T(8,128)S(1)}, u32[]{:S(2)}) copy-start(f32[512,128]{1,0:T(8,128)S(1)} %fusion.303) | copy-start | bytes 786436
  953.6 6.8 collective-permute-start.8
  991.2 10.1 collective-permute-start.9
  1131.1 47.6 %copy-start.4 = (f32[256,512]{1,0:T(8,128)S(1)}, f32[256,512]{1,0:T(8,128)}, u32[]{:S(2)}) copy-start(f32[256,512]{1,0:T(8,128)} %gather_fusion.96) | copy-start | bytes 1572868
  1131.1 47.6 %copy-start.217 = (pred[256]{0:T(512)(128)(4,1)S(1)}, pred[256]{0:T(512)(128)(4,1)}, u32[]{:S(2)}) copy-start(pred[256]{0:T(512)(128)(4,1)} %get-tuple-element.147) | copy-start | bytes 772
  (237 other events, 1089.9 us)
Sparse Core Ops, SparseCore 0:
  15.2 47.2 all-gather.10
  233.4 41.2 all-gather.12
  445.0 41.2 all-gather.14
  660.7 42.0 all-gather.16
  885.3 39.5 all-gather.18
where the time goes:
time: 1210 us; the launch traced here: 1200 us
  other arithmetic  596 us (49%)
  local copies, waits for them, and re-layouts  231 us (19%)
  blocking collectives  128 us (11%)
  matrix products  110 us (9%)
  waiting for transfers between devices  75.7 us (6%)
  starting transfers between devices  39.8 us (3%)
  between operations  23.6 us (2%)
    another operation x240, other arithmetic, factor_inverse(): lower_factor = jnp.linalg.cholesky(matrix)  291 us
    another operation x160, other arithmetic, factor_inverse(): return jax.scipy.linalg.solve_triangular(lower_factor, identity, lower=True)  247 us
    all_gather x5, blocking collectives, per_device(): lax.all_gather(jnp.stack([rhs_blk, other_rhs]), 'row', axis=1, tiled=True)  128 us
    dot_general x325, matrix products, matmul_high(): return jnp.dot(left, right, precision=lax.Precision.HIGHEST)  91 us
    gather x50, local copies, waits for them, and re-layouts, spread_block(): jnp.take(jnp.take(full_matrix, jnp.maximum(src_rows, 0), axis=0), jnp.max...  60.6 us
    all_gather x5, waiting for transfers between devices, per_device(): lax.all_gather(jnp.stack([update_blk, other_upd])[:, None], ('row', 'col'...  46.7 us
    gather x30, local copies, waits for them, and re-layouts, spread_block(): jnp.take(full_matrix, jnp.maximum(src_rows, 0), axis=0)  41.8 us
    ppermute x10, starting transfers between devices, from_partner(): return lax.ppermute(block, axis, route)  39.6 us
  transfers between devices with their start and end apart: 15, of which 11 were waited for; matrix products, arithmetic and copies ran while one was open for 37% of the time, Pallas kernels for 0%

commit v1 on v0

--- a/solution.py
+++ b/solution.py
@@ -92,7 +92,12 @@
         blocks = lax.all_gather(
             jnp.stack([update_blk, other_upd])[:, None], ("row", "col"), axis=1, tiled=True
         )
-        whole_rhs = lax.all_gather(jnp.stack([rhs_blk, other_rhs]), "row", axis=1, tiled=True)
+        whole_rhs = jnp.concatenate(
+            lax.all_to_all(
+                jnp.stack([jnp.stack([rhs_blk, other_rhs])] * lax.axis_size("row")), "row", 0, 0
+            ),
+            axis=1,
+        )
         whole_upd = (
             blocks.reshape(2, row_count, col_count, row_block, col_block)
             .transpose(0, 1, 3, 2, 4)

time: 1210 us -> 1160 us (0.959)
  blocking collectives: 128 us -> 0 us
  waiting for transfers between devices: 75.7 us -> 129 us
  starting transfers between devices: 39.8 us -> 63.7 us
    all_gather x5 -> x0, blocking collectives: 128 us -> none  [per_device(): lax.all_gather(jnp.stack([rhs_blk, other_rhs]), 'row', axis=1, tiled=True)]
    all_to_all x0 -> x5, waiting for transfers between devices: none -> 41.2 us  [per_device(): lax.all_to_all(jnp.stack([jnp.stack([rhs_blk, other_rhs])] * lax.axis_siz...]
    all_to_all x0 -> x5, starting transfers between devices: none -> 23.2 us  [per_device(): lax.all_to_all(jnp.stack([jnp.stack([rhs_blk, other_rhs])] * lax.axis_siz...]
    all_gather x5, waiting for transfers between devices: 46.7 us -> 60.6 us  [per_device(): lax.all_gather(jnp.stack([update_blk, other_upd])[:, None], ('row', 'col'...]
  transfers between devices with their start and end apart: 15 -> 20, of which waited for: 11 -> 15; matrix products, arithmetic and copies ran while one was open for 37% -> 39% of each run, Pallas kernels for 0% -> 0%
where the time goes in v1:
time: 1160 us; the launch traced here: 1150 us
  other arithmetic  592 us (51%)
  local copies, waits for them, and re-layouts  234 us (20%)
  waiting for transfers between devices  129 us (11%)
  matrix products  109 us (9%)
  starting transfers between devices  63.7 us (5%)
  between operations  23.5 us (2%)
    another operation x240, other arithmetic, factor_inverse(): lower_factor = jnp.linalg.cholesky(matrix)  290 us
    another operation x160, other arithmetic, factor_inverse(): return jax.scipy.linalg.solve_triangular(lower_factor, identity, lower=True)  245 us
    dot_general x325, matrix products, matmul_high(): return jnp.dot(left, right, precision=lax.Precision.HIGHEST)  90.4 us
    all_gather x5, waiting for transfers between devices, per_device(): lax.all_gather(jnp.stack([update_blk, other_upd])[:, None], ('row', 'col'...  60.6 us
    gather x50, local copies, waits for them, and re-layouts, spread_block(): jnp.take(jnp.take(full_matrix, jnp.maximum(src_rows, 0), axis=0), jnp.max...  60.6 us
    gather x30, local copies, waits for them, and re-layouts, spread_block(): jnp.take(full_matrix, jnp.maximum(src_rows, 0), axis=0)  41.8 us
    all_to_all x5, waiting for transfers between devices, per_device(): lax.all_to_all(jnp.stack([jnp.stack([rhs_blk, other_rhs])] * lax.axis_siz...  41.2 us
    ppermute x10, starting transfers between devices, from_partner(): return lax.ppermute(block, axis, route)  40.2 us
  transfers between devices with their start and end apart: 20, of which 15 were waited for; matrix products, arithmetic and copies ran while one was open for 39% of the time, Pallas kernels for 0%

profile of v1, /device:TPU:56, one launch (start us, length us, event | category | flops | bytes accessed | tf_op | source)
XLA Modules:
  0.0 1151.3 jit_solution(4540124459350738485)
XLA Ops:
  7.2 3.4 collective-permute-start
  10.6 3.0 collective-permute-done
  35.2 27.3 %all-gather.11.cloned.1.call-done = f32[2,1024,256]{2,1,0:T(8,128)} async-done(((f32[2,64,256]{2,1,0:T(8,128)}), f32[2,1024,256]{2,1,0:T(8,128)}) %all-gather.11.cloned.1.call-update) | async-done | bytes 2097168 | tf_op jit(solution)/shard_map/all_gather | solution.py:92
  62.5 3.2 copy.795
  98.7 2.9 cholesky.1225
  130.2 2.9 cholesky.1269
  145.7 2.9 cholesky.1291
  178.1 3.1 cholesky.1335
  194.2 2.9 cholesky.1357
  225.0 4.9 collective-permute-start.1
  261.9 12.9 %all-gather.13.cloned.1.call-done = f32[2,1024,256]{2,1,0:T(8,128)} async-done(((f32[2,64,256]{2,1,0:T(8,128)}), f32[2,1024,256]{2,1,0:T(8,128)}) %all-gather.13.cloned.1.call-update) | async-done | bytes 2097168 | tf_op jit(solution)/shard_map/all_gather | solution.py:92
  311.2 2.9 cholesky.1401
  342.3 2.9 cholesky.1445
  357.7 2.9 cholesky.1467
  375.2 2.9 cholesky.1489
  390.6 3.1 cholesky.1511
  406.5 2.9 cholesky.1533
  437.1 3.4 collective-permute-start.2
  443.9 3.4 collective-permute-start.5
  465.0 20.4 %all-gather.15.cloned.1.call-done = f32[2,1024,256]{2,1,0:T(8,128)} async-done(((f32[2,64,256]{2,1,0:T(8,128)}), f32[2,1024,256]{2,1,0:T(8,128)}) %all-gather.15.cloned.1.call-update) | async-done | bytes 2097168 | tf_op jit(solution)/shard_map/all_gather | solution.py:92
  521.7 2.9 cholesky.1577
  552.8 2.9 cholesky.1621
  601.0 3.1 cholesky.1687
  616.8 2.9 cholesky.1709
  647.6 4.2 collective-permute-start.3
  653.5 4.2 all-to-all-start
  668.3 7.0 all-to-all-done
  681.1 4.9 collective-permute-start.6
  689.3 3.5 all-to-all-start.1
  701.3 8.3 all-to-all-done.1
  715.5 3.4 collective-permute-start.7
  722.2 4.1 all-to-all-start.2
  761.7 2.9 cholesky.1753
  809.2 2.9 cholesky.1819
  842.7 3.1 cholesky.1863
  889.9 4.3 collective-permute-start.4
  894.2 5.7 collective-permute-done.4
  907.1 3.3 collective-permute-start.8
  910.3 3.4 collective-permute-done.8
  914.6 7.5 all-to-all-start.3
  926.8 13.3 %all-to-all-done.3 = f32[8,2,64,128]{3,2,1,0:T(8,128)S(1)} async-done(((f32[8,2,64,128]{3,2,1,0:T(8,128)}), f32[8,2,64,128]{3,2,1,0:T(8,128)S(1)}, u32[]{:S(2)}, u32[]{:S(2)}) %all-to-all-start.3) | async-done | bytes 524320 | tf_op jit(solution)/shard_map/all_to_all | solution.py:96
  945.6 5.2 collective-permute-start.9
  950.8 4.5 collective-permute-done.9
  956.2 4.0 all-to-all-start.4
  960.8 12.7 %all-to-all-done.4 = f32[8,2,64,128]{3,2,1,0:T(8,128)S(1)} async-done(((f32[8,2,64,128]{3,2,1,0:T(8,128)}), f32[8,2,64,128]{3,2,1,0:T(8,128)S(1)}, u32[]{:S(2)}, u32[]{:S(2)}) %all-to-all-start.4) | async-done | bytes 524320 | tf_op jit(solution)/shard_map/all_to_all | solution.py:96
  1014.2 2.9 cholesky.1929
  1078.0 2.9 cholesky.2017
  1093.6 3.1 cholesky.2039
  (1910 shorter events, 880.4 us)
Async XLA Ops:
  7.2 55.3 %all-gather.11.cloned.1.call-start = ((), (), s32[]{:S(2)}) async-start(), calls=%async_computation.5 | async-start | bytes 2228224 | tf_op jit(solution)/shard_map/all_gather | solution.py:92
  7.2 6.4 collective-permute-start
  15.1 259.7 %all-gather.13.cloned.1.call-start = ((), (), s32[]{:S(2)}) async-start(), calls=%async_computation.6 | async-start | bytes 2228224 | tf_op jit(solution)/shard_map/all_gather | solution.py:92
  32.0 178.2 %copy-start.87 = (s32[1024]{0:T(1024)}, s32[1024]{0:T(1024)S(1)}, u32[]{:S(2)}) copy-start(s32[1024]{0:T(1024)S(1)} %pad_clamp_fusion.25) | copy-start | bytes 12292
  32.0 34.7 %copy-start.136 = (s32[1024]{0:T(1024)}, s32[1024]{0:T(1024)S(1)}, u32[]{:S(2)}) copy-start(s32[1024]{0:T(1024)S(1)} %pad_clamp_fusion.30) | copy-start | bytes 12292
  34.1 33.3 %copy-start.186 = (pred[64]{0:T(512)(128)(4,1)}, pred[64]{0:T(512)(128)(4,1)S(1)}, u32[]{:S(2)}) copy-start(pred[64]{0:T(512)(128)(4,1)S(1)} %get-tuple-element.163) | copy-start | bytes 196
  153.4 69.8 %copy-start.25 = (f32[256,256]{1,0:T(8,128)}, f32[256,256]{1,0:T(8,128)S(1)}, u32[]{:S(2)}) copy-start(f32[256,256]{1,0:T(8,128)S(1)} %select_maximum_fusion.9) | copy-start | bytes 786436
  154.9 54.8 %copy-start.24 = (f32[256,64]{1,0:T(8,128)S(1)}, f32[256,64]{1,0:T(8,128)}, u32[]{:S(2)}) copy-start(f32[256,64]{1,0:T(8,128)} %gather_fusion.33) | copy-start | bytes 196612
  162.6 47.3 %copy-start = (f32[256,512]{1,0:T(8,128)S(1)}, f32[256,512]{1,0:T(8,128)}, u32[]{:S(2)}) copy-start(f32[256,512]{1,0:T(8,128)} %gather_fusion.40) | copy-start | bytes 1572868
  162.6 47.3 %copy-start.209 = (pred[256]{0:T(512)(128)(4,1)S(1)}, pred[256]{0:T(512)(128)(4,1)}, u32[]{:S(2)}) copy-start(pred[256]{0:T(512)(128)(4,1)} %get-tuple-element.143) | copy-start | bytes 772
  225.0 7.7 collective-permute-start.1
  233.4 252.0 %all-gather.15.cloned.1.call-start = ((), (), s32[]{:S(2)}) async-start(), calls=%async_computation.7 | async-start | bytes 2228224 | tf_op jit(solution)/shard_map/all_gather | solution.py:92
  250.0 26.5 %copy-start.127 = (s32[256]{0:T(256)}, s32[256]{0:T(256)S(1)}, u32[]{:S(2)}) copy-start(s32[256]{0:T(256)S(1)} %gather_fusion.19) | copy-start | bytes 3076
  365.3 69.9 %copy-start.29 = (f32[256,256]{1,0:T(8,128)}, f32[256,256]{1,0:T(8,128)S(1)}, u32[]{:S(2)}) copy-start(f32[256,256]{1,0:T(8,128)S(1)} %select_maximum_fusion.8) | copy-start | bytes 786436
  367.5 54.3 %copy-start.18 = (f32[256,64]{1,0:T(8,128)S(1)}, f32[256,64]{1,0:T(8,128)}, u32[]{:S(2)}) copy-start(f32[256,64]{1,0:T(8,128)} %gather_fusion.45) | copy-start | bytes 196612
  374.8 47.2 %copy-start.1 = (f32[256,512]{1,0:T(8,128)S(1)}, f32[256,512]{1,0:T(8,128)}, u32[]{:S(2)}) copy-start(f32[256,512]{1,0:T(8,128)} %gather_fusion.54) | copy-start | bytes 1572868
  374.8 47.2 %copy-start.207 = (pred[256]{0:T(512)(128)(4,1)S(1)}, pred[256]{0:T(512)(128)(4,1)}, u32[]{:S(2)}) copy-start(pred[256]{0:T(512)(128)(4,1)} %get-tuple-element.82) | copy-start | bytes 772
  398.6 23.6 %copy-start.97 = (s32[1024]{0:T(1024)S(1)}, s32[1024]{0:T(1024)}, u32[]{:S(2)}) copy-start(s32[1024]{0:T(1024)} %copy-done.95) | copy-start | bytes 12292
  437.1 6.2 collective-permute-start.2
  443.9 207.9 %collective-permute-start.5 = (f32[64,128]{1,0:T(8,128)}, f32[64,128]{1,0:T(8,128)}, u32[]{:S(2)}, u32[]{:S(2)}) collective-permute-start(f32[64,128]{1,0:T(8,128)} %bitcast.331), channel_id=1, source_target_pairs={{0,16},{16,0},{32,48},{48,32},{64,80},{80,64},{96,112},{112,96},{1... | collective-permute-start | bytes 98312 | tf_op jit(solution)/shard_map/ppermute | solution.py:14
  457.1 30.1 %copy-start.113 = (s32[512]{0:T(512)}, s32[512]{0:T(512)S(1)}, u32[]{:S(2)}) copy-start(s32[512]{0:T(512)S(1)} %gather_fusion.24) | copy-start | bytes 6148
  462.0 25.2 %copy-start.115 = (s32[512]{0:T(512)}, s32[512]{0:T(512)S(1)}, u32[]{:S(2)}) copy-start(s32[512]{0:T(512)S(1)} %gather_fusion.25) | copy-start | bytes 6148
  463.8 28.3 %copy-start.99 = (s32[1024]{0:T(1024)}, s32[1024]{0:T(1024)S(1)}, u32[]{:S(2)}) copy-start(s32[1024]{0:T(1024)S(1)} %pad_clamp_fusion.13) | copy-start | bytes 12292
  463.8 24.2 %copy-start.138 = (s32[1024]{0:T(1024)}, s32[1024]{0:T(1024)S(1)}, u32[]{:S(2)}) copy-start(s32[1024]{0:T(1024)S(1)} %pad_clamp_fusion.17) | copy-start | bytes 12292
  575.8 69.9 %copy-start.27 = (f32[256,256]{1,0:T(8,128)}, f32[256,256]{1,0:T(8,128)S(1)}, u32[]{:S(2)}) copy-start(f32[256,256]{1,0:T(8,128)S(1)} %select_maximum_fusion.7) | copy-start | bytes 786436
  578.0 54.2 %copy-start.19 = (f32[256,64]{1,0:T(8,128)S(1)}, f32[256,64]{1,0:T(8,128)}, u32[]{:S(2)}) copy-start(f32[256,64]{1,0:T(8,128)} %gather_fusion.59) | copy-start | bytes 196612
  585.2 47.1 %copy-start.2 = (f32[256,512]{1,0:T(8,128)S(1)}, f32[256,512]{1,0:T(8,128)}, u32[]{:S(2)}) copy-start(f32[256,512]{1,0:T(8,128)} %gather_fusion.68) | copy-start | bytes 1572868
  585.2 47.1 %copy-start.203 = (pred[256]{0:T(512)(128)(4,1)S(1)}, pred[256]{0:T(512)(128)(4,1)}, u32[]{:S(2)}) copy-start(pred[256]{0:T(512)(128)(4,1)} %get-tuple-element.145) | copy-start | bytes 772
  647.6 10.1 collective-permute-start.3
  653.5 21.8 %all-to-all-start = ((f32[8,2,64,128]{3,2,1,0:T(8,128)}), f32[8,2,64,128]{3,2,1,0:T(8,128)S(1)}, u32[]{:S(2)}, u32[]{:S(2)}) async-start(f32[8,2,64,128]{3,2,1,0:T(8,128)} %stack.155), calls=%async_computation | async-start | bytes 1048576 | tf_op jit(solution)/shard_map/all_to_all | solution.py:96
  657.6 68.7 %all-gather.17.cloned.1.call-start = ((), (), s32[]{:S(2)}) async-start(), calls=%async_computation.8 | async-start | bytes 2228224 | tf_op jit(solution)/shard_map/all_gather | solution.py:92
  668.3 61.4 %copy-start.196 = (pred[64]{0:T(512)(128)(4,1)}, pred[64]{0:T(512)(128)(4,1)S(1)}, u32[]{:S(2)}) copy-start(pred[64]{0:T(512)(128)(4,1)S(1)} %get-tuple-element.94) | copy-start | bytes 196
  681.1 7.3 collective-permute-start.6
  686.0 48.1 %copy-start.104 = (s32[1024]{0:T(1024)}, s32[1024]{0:T(1024)S(1)}, u32[]{:S(2)}) copy-start(s32[1024]{0:T(1024)S(1)} %pad_clamp_fusion.7) | copy-start | bytes 12292
  689.3 20.3 %all-to-all-start.1 = ((f32[8,2,64,128]{3,2,1,0:T(8,128)}), f32[8,2,64,128]{3,2,1,0:T(8,128)S(1)}, u32[]{:S(2)}, u32[]{:S(2)}) async-start(f32[8,2,64,128]{3,2,1,0:T(8,128)} %stack.159), calls=%async_computation.1 | async-start | bytes 1048576 | tf_op jit(solution)/shard_map/all_to_all | solution.py:96
  715.5 5.8 collective-permute-start.7
  722.2 178.5 %all-to-all-start.2 = ((f32[8,2,64,128]{3,2,1,0:T(8,128)}), f32[8,2,64,128]{3,2,1,0:T(8,128)}, u32[]{:S(2)}, u32[]{:S(2)}) async-start(f32[8,2,64,128]{3,2,1,0:T(8,128)} %stack.163), calls=%async_computation.2 | async-start | bytes 1048576 | tf_op jit(solution)/shard_map/all_to_all | solution.py:96
  726.3 252.9 %all-gather.19.cloned.1.call-start = ((), (), s32[]{:S(2)}) async-start(), calls=%async_computation.9 | async-start | bytes 2228224 | tf_op jit(solution)/shard_map/all_gather | solution.py:92
  826.6 48.2 %copy-start.3 = (f32[256,512]{1,0:T(8,128)S(1)}, f32[256,512]{1,0:T(8,128)}, u32[]{:S(2)}) copy-start(f32[256,512]{1,0:T(8,128)} %gather_fusion.82) | copy-start | bytes 1572868
  826.6 48.2 %copy-start.205 = (pred[256]{0:T(512)(128)(4,1)S(1)}, pred[256]{0:T(512)(128)(4,1)}, u32[]{:S(2)}) copy-start(pred[256]{0:T(512)(128)(4,1)} %get-tuple-element.74) | copy-start | bytes 772
  850.9 24.1 %copy-start.106 = (s32[1024]{0:T(1024)S(1)}, s32[1024]{0:T(1024)}, u32[]{:S(2)}) copy-start(s32[1024]{0:T(1024)} %copy-done.104) | copy-start | bytes 12292
  889.9 10.1 collective-permute-start.4
  907.1 6.7 collective-permute-start.8
  914.6 25.4 %all-to-all-start.3 = ((f32[8,2,64,128]{3,2,1,0:T(8,128)}), f32[8,2,64,128]{3,2,1,0:T(8,128)S(1)}, u32[]{:S(2)}, u32[]{:S(2)}) async-start(f32[8,2,64,128]{3,2,1,0:T(8,128)} %stack.167), calls=%async_computation.3 | async-start | bytes 1048576 | tf_op jit(solution)/shard_map/all_to_all | solution.py:96
  945.6 9.7 collective-permute-start.9
  956.2 17.4 %all-to-all-start.4 = ((f32[8,2,64,128]{3,2,1,0:T(8,128)}), f32[8,2,64,128]{3,2,1,0:T(8,128)S(1)}, u32[]{:S(2)}, u32[]{:S(2)}) async-start(f32[8,2,64,128]{3,2,1,0:T(8,128)} %stack.171), calls=%async_computation.4 | async-start | bytes 1048576 | tf_op jit(solution)/shard_map/all_to_all | solution.py:96
  1077.6 47.6 %copy-start.4 = (f32[256,512]{1,0:T(8,128)S(1)}, f32[256,512]{1,0:T(8,128)}, u32[]{:S(2)}) copy-start(f32[256,512]{1,0:T(8,128)} %gather_fusion.96) | copy-start | bytes 1572868
  1077.6 47.6 %copy-start.201 = (pred[256]{0:T(512)(128)(4,1)S(1)}, pred[256]{0:T(512)(128)(4,1)}, u32[]{:S(2)}) copy-start(pred[256]{0:T(512)(128)(4,1)} %get-tuple-element.147) | copy-start | bytes 772
  (227 other events, 1094.6 us)
Sparse Core Ops, SparseCore 0:
  15.2 47.2 all-gather.10
  233.5 41.2 all-gather.12
  444.0 41.2 all-gather.14
  660.3 44.5 all-gather.16
  900.7 47.7 all-gather.18
